TPU v7x, 32 devices: a whole 2x2x4 slice. The times are simulated.
32 devices in a mesh: groups: 2 (over y), expert: 8 (over z, x), tensor: 2 (over core).
Axes of the slice: x: 2, y: 2, z: 4, core: 2. Of those that a mesh axis runs over, the one named last changes fastest.
Arguments:
- tokens: bfloat16 [128, 6144], P(('groups', 'expert'), 'tensor'), parts along dimension 0, may hold values from -6 to 6
- grad_out: bfloat16 [128, 6144], P(('groups', 'expert'), 'tensor'), parts along dimension 0, may hold values from -6 to 6
- gate_weight: bfloat16 [6144, 16384], P('tensor', 'expert'), may hold values from -0.078125 to 0.078125
- up_weight: bfloat16 [6144, 16384], P('tensor', 'expert'), may hold values from -0.078125 to 0.078125
- down_weight: bfloat16 [16384, 6144], P('expert', 'tensor'), may hold values from -0.0625 to 0.0625
- counts: int32 [16, 2], P(('groups', 'expert')), parts along dimension 0, may hold values from 0 to 2, as said below
- slot_token: int32 [16, 2, 2], P(('groups', 'expert')), parts along dimension 0, may hold values from 0 to 7, as said below
- gates: float32 [16, 2, 2], P(('groups', 'expert')), parts along dimension 0, may hold values from 0.25 to 1
Outputs:
- mixed: bfloat16 [128, 6144], P(('groups', 'expert'), 'tensor'), parts along dimension 0
- grad_tokens: bfloat16 [128, 6144], P(('groups', 'expert'), 'tensor'), parts along dimension 0
- grad_gate: bfloat16 [12288, 16384], P(('groups', 'tensor'), 'expert'), parts along dimension 0
- grad_up: bfloat16 [12288, 16384], P(('groups', 'tensor'), 'expert'), parts along dimension 0
- grad_down: bfloat16 [32768, 6144], P(('groups', 'expert'), 'tensor'), parts along dimension 0
There are 2 independent parts, one for each index of `groups`. A program takes and returns all parts, laid end to end along the dimension named above; an argument that names none is the same for every part. Nothing has to cross between parts.
Inputs may be any that keep to these rules, and one draw needn't show every extreme that they name: `counts`: some expert has all 2 slots used by every owner. `slot_token`: the 2 slots of one owner and one expert name distinct tokens.
All inputs are finite; a program needn't handle non-finite values.
Results may differ from a plain program's by a relative error of at most 0.0059.
Values may be sent and summed in bfloat16 or wider, within the bound.
A program may use at most 192 MiB of HBM per device.

v0:
```python
import jax
import jax.numpy as jnp
from jax import lax
from jax.sharding import PartitionSpec as P

ACTIVE_EXPERTS = 2
SLOT_CAPACITY = 2


def shards(tokens, grad_out, gate_weight, up_weight, down_weight, counts, slot_token, gates):
    holder_devices = lax.axis_size("expert")
    device_subset = holder_devices // ACTIVE_EXPERTS
    tok_dev = tokens.shape[0]
    column_range = tokens.shape[1]
    filled_slots = ACTIVE_EXPERTS * SLOT_CAPACITY
    live_slots = (
        (lax.broadcasted_iota(jnp.int32, (ACTIVE_EXPERTS, SLOT_CAPACITY), 1) < counts[0][:, None])
        .astype(jnp.float32)
        .reshape(filled_slots)
    )
    choose = (
        slot_token[0].reshape(filled_slots)[:, None]
        == lax.broadcasted_iota(jnp.int32, (filled_slots, tok_dev), 1)
    ).astype(jnp.float32)
    choose = choose * live_slots[:, None]
    choose_half = choose.astype(jnp.bfloat16)
    slot_gates = gates[0].reshape(filled_slots)
    packed_x = (
        jnp.dot(choose_half, tokens, preferred_element_type=jnp.float32)
        .astype(jnp.bfloat16)
        .reshape(ACTIVE_EXPERTS, SLOT_CAPACITY, column_range)
    )
    gathered_gradient = (
        jnp.dot(choose_half, grad_out, preferred_element_type=jnp.float32) * slot_gates[:, None]
    ).astype(jnp.bfloat16)
    gathered_gradient = gathered_gradient.reshape(ACTIVE_EXPERTS, SLOT_CAPACITY, column_range)
    arrived_x, arrived_grad = (
        lax.all_to_all(
            jnp.repeat(packed_x, device_subset, axis=0),
            "expert",
            split_axis=0,
            concat_axis=0,
            tiled=True,
        ),
        lax.all_to_all(
            jnp.repeat(gathered_gradient, device_subset, axis=0),
            "expert",
            split_axis=0,
            concat_axis=0,
            tiled=True,
        ),
    )
    rows_x = arrived_x.reshape(holder_devices * SLOT_CAPACITY, column_range)
    rows_grad = arrived_grad.reshape(holder_devices * SLOT_CAPACITY, column_range)
    pre_gate = jnp.dot(rows_x, gate_weight, preferred_element_type=jnp.float32)
    pre_up = jnp.dot(rows_x, up_weight, preferred_element_type=jnp.float32)
    grad_hidden = jnp.einsum(
        "rd,hd->rh", rows_grad, down_weight, preferred_element_type=jnp.float32
    )
    pre_gate, pre_up, grad_hidden = lax.psum((pre_gate, pre_up, grad_hidden), "tensor")
    gate_sig = jax.nn.sigmoid(pre_gate)
    active = (pre_gate * gate_sig * pre_up).astype(jnp.bfloat16)
    out_part = jnp.dot(active, down_weight, preferred_element_type=jnp.float32).reshape(
        holder_devices, SLOT_CAPACITY, column_range
    )
    grad_upin = (grad_hidden * pre_gate * gate_sig).astype(jnp.bfloat16)
    grad_gatein = (grad_hidden * pre_up * gate_sig * (1.0 + pre_gate * (1.0 - gate_sig))).astype(
        jnp.bfloat16
    )
    back_part = jnp.einsum(
        "rh,dh->rd", grad_gatein, gate_weight, preferred_element_type=jnp.float32
    )
    back_part = back_part + jnp.einsum(
        "rh,dh->rd", grad_upin, up_weight, preferred_element_type=jnp.float32
    )
    back_part = back_part.reshape(holder_devices, SLOT_CAPACITY, column_range)
    output_returned, returned_gradient = (
        lax.all_to_all(out_part, "expert", split_axis=0, concat_axis=0, tiled=True),
        lax.all_to_all(back_part, "expert", split_axis=0, concat_axis=0, tiled=True),
    )
    grad_gate = jnp.einsum(
        "rd,rh->dh", rows_x, grad_gatein, preferred_element_type=jnp.float32
    ).astype(jnp.bfloat16)
    grad_up = jnp.einsum("rd,rh->dh", rows_x, grad_upin, preferred_element_type=jnp.float32).astype(
        jnp.bfloat16
    )
    grad_down = jnp.einsum(
        "rh,rd->hd", active, rows_grad, preferred_element_type=jnp.float32
    ).astype(jnp.bfloat16)
    out_slots = (
        output_returned.reshape(ACTIVE_EXPERTS, device_subset, SLOT_CAPACITY, column_range)
        .sum(axis=1)
        .reshape(filled_slots, column_range)
    )
    back_slots = (
        returned_gradient.reshape(ACTIVE_EXPERTS, device_subset, SLOT_CAPACITY, column_range)
        .sum(axis=1)
        .reshape(filled_slots, column_range)
    )
    mixed_weights = choose * slot_gates[:, None]
    mixed = jnp.sum(mixed_weights[:, :, None] * out_slots[:, None, :], axis=0)
    grad_tokens = jnp.sum(choose[:, :, None] * back_slots[:, None, :], axis=0)
    return (
        mixed.astype(jnp.bfloat16),
        grad_tokens.astype(jnp.bfloat16),
        grad_gate,
        grad_up,
        grad_down,
    )


def solution(mesh):
    in_specs = (
        P(("groups", "expert"), "tensor"),
        P(("groups", "expert"), "tensor"),
        P("tensor", "expert"),
        P("tensor", "expert"),
        P("expert", "tensor"),
        P(("groups", "expert"), None),
        P(("groups", "expert"), None, None),
        P(("groups", "expert"), None, None),
    )
    out_specs = (
        P(("groups", "expert"), "tensor"),
        P(("groups", "expert"), "tensor"),
        P(("groups", "tensor"), "expert"),
        P(("groups", "tensor"), "expert"),
        P(("groups", "expert"), "tensor"),
    )
    return jax.shard_map(shards, mesh=mesh, in_specs=in_specs, out_specs=out_specs, check_vma=False)
```

profile of v0, /device:TPU:0, one launch (start us, length us, event | category | flops | bytes accessed | tf_op | source)
XLA Modules:
  0.0 129.3 jit_solution(9305271163034542061)
XLA Ops:
  7.2 0.8 eq.17
  8.0 0.7 compare_convert_fusion
  8.7 0.1 reshape.159
  8.8 0.2 convolution_convert_fusion.3
  9.0 0.7 broadcast_in_dim.8
  9.7 7.3 %all-to-all-start = ((bf16[8,2,3072]{2,1,0:T(2,128)(2,1)}), bf16[8,2,3072]{2,1,0:T(2,128)(2,1)S(1)}, u32[]{:S(2)}, u32[]{:S(2)}) async-start(bf16[8,2,3072]{2,1,0:T(2,128)(2,1)} %bitcast.1), calls=%async_computation | async-start | bytes 196608 | tf_op jit(solution)/shard_map/all_to_all | solution.py:38
  16.9 0.8 mul.86
  17.7 1.0 fusion
  18.7 5.3 %all-to-all-done = bf16[8,2,3072]{2,1,0:T(2,128)(2,1)S(1)} async-done(((bf16[8,2,3072]{2,1,0:T(2,128)(2,1)}), bf16[8,2,3072]{2,1,0:T(2,128)(2,1)S(1)}, u32[]{:S(2)}, u32[]{:S(2)}) %all-to-all-start) | async-done | bytes 98336 | tf_op jit(solution)/shard_map/all_to_all | solution.py:38
  24.1 0.7 broadcast_in_dim.9
  24.8 3.4 %all-to-all-start.2 = ((bf16[8,2,3072]{2,1,0:T(2,128)(2,1)}), bf16[8,2,3072]{2,1,0:T(2,128)(2,1)S(1)}, u32[]{:S(2)}, u32[]{:S(2)}) async-start(bf16[8,2,3072]{2,1,0:T(2,128)(2,1)} %bitcast.3), calls=%async_computation.2 | async-start | bytes 196608 | tf_op jit(solution)/shard_map/all_to_all | solution.py:45
  28.2 7.1 %fusion.15 = f32[16,2048]{1,0:T(8,128)} fusion(bf16[16,3072]{1,0:T(8,128)(2,1)S(1)} %reshape.151, bf16[3072,2048]{1,0:T(8,128)(2,1)} %param.11), kind=kOutput, calls=%fused_computation.29 | convolution fusion | flops 201326592 | bytes 12812288 | tf_op jit(solution)/shard_map/dot_general | solution.py:56
  35.4 1.1 copy-done.2
  36.4 2.4 %fusion.14 = f32[16,2048]{1,0:T(8,128)} fusion(bf16[16,3072]{1,0:T(8,128)(2,1)S(1)} %reshape.151, bf16[3072,2048]{1,0:T(8,128)(2,1)S(1)} %copy-done.2), kind=kOutput, calls=%fused_computation.28 | convolution fusion | flops 201326592 | bytes 12812288 | tf_op jit(solution)/shard_map/dot_general | solution.py:55
  38.9 8.6 %fusion.17 = f32[16,2048]{1,0:T(8,128)} fusion(bf16[16,3072]{1,0:T(8,128)(2,1)S(1)} %reshape.156, bf16[2048,3072]{1,0:T(8,128)(2,1)} %param.12), kind=kOutput, calls=%fused_computation.31 | convolution fusion | flops 201326592 | bytes 12812288 | tf_op jit(solution)/shard_map/rd,hd->rh/dot_general | solution.py:57
  47.5 0.1 fusion.1
  47.6 20.0 %all-reduce.3.cloned.1.call-done = (f32[16,2048]{1,0:T(8,128)}, f32[16,2048]{1,0:T(8,128)}, f32[16,2048]{1,0:T(8,128)}) async-done(((f32[16,2048]{1,0:T(8,128)}, f32[16,2048]{1,0:T(8,128)}, f32[16,2048]{1,0:T(8,128)}), (f32[16,2048]{1,0:T(8,128)}, f32[16,2048]{1,0:T(8,128)}, f32[16,2048]{1,0:T(8,128)})) %all-reduce.3.cloned.1.call-update) | async-done | bytes 393232 | tf_op jit(solution)/shard_map/psum | solution.py:60
  67.6 1.1 multiply_convert_fusion
  68.7 7.9 %fusion.18 = f32[16,3072]{1,0:T(8,128)S(1)} fusion(bf16[16,2048]{1,0:T(8,128)(2,1)S(1)} %get-tuple-element.9, bf16[3072,2048]{1,0:T(8,128)(2,1)} %param.10), kind=kOutput, calls=%fused_computation.32 | convolution fusion | flops 201326592 | bytes 12845056 | tf_op jit(solution)/shard_map/rh,dh->rd/dot_general | solution.py:70
  76.6 6.8 %convolution_convert_fusion.2 = bf16[3072,2048]{1,0:T(8,128)(2,1)} fusion(bf16[16,3072]{1,0:T(8,128)(2,1)S(1)} %reshape.151, bf16[16,2048]{1,0:T(8,128)(2,1)S(1)} %get-tuple-element.9), kind=kOutput, calls=%fused_computation.2 | convolution fusion | flops 207618048 | bytes 12746752 | tf_op jit(solution)/shard_map/rd,rh->dh/dot_general | solution.py:81
  83.4 6.6 %convolution_convert_fusion.1 = bf16[3072,2048]{1,0:T(8,128)(2,1)} fusion(bf16[16,3072]{1,0:T(8,128)(2,1)S(1)} %reshape.151, bf16[16,2048]{1,0:T(8,128)(2,1)S(1)} %get-tuple-element.8), kind=kOutput, calls=%fused_computation.1 | convolution fusion | flops 207618048 | bytes 12746752 | tf_op jit(solution)/shard_map/rd,rh->dh/dot_general | solution.py:84
  90.0 3.3 %convolution_add_fusion = f32[16,3072]{1,0:T(8,128)S(1)} fusion(f32[16,3072]{1,0:T(8,128)S(1)} %fusion.18, bf16[16,2048]{1,0:T(8,128)(2,1)S(1)} %get-tuple-element.8, bf16[3072,2048]{1,0:T(8,128)(2,1)S(1)} %bitcast.28), kind=kOutput, calls=%fused_computation.3 | convolution fusion | flops 201375744 | bytes 13041664 | tf_op jit(solution)/shard_map/rh,dh->rd/dot_general | solution.py:73
  93.4 0.8 reshape.157
  94.2 5.8 %all-to-all-start.3 = ((f32[8,2,3072]{2,1,0:T(2,128)}), f32[8,2,3072]{2,1,0:T(2,128)S(1)}, u32[]{:S(2)}, u32[]{:S(2)}) async-start(f32[8,2,3072]{2,1,0:T(2,128)} %reshape.157), calls=%async_computation.3 | async-start | bytes 393216 | tf_op jit(solution)/shard_map/all_to_all | solution.py:79
  100.0 6.3 %fusion.16 = f32[16,3072]{1,0:T(8,128)S(1)} fusion(bf16[16,2048]{1,0:T(8,128)(2,1)S(1)} %get-tuple-element.10, bf16[2048,3072]{1,0:T(8,128)(2,1)} %param.12), kind=kOutput, calls=%fused_computation.30 | convolution fusion | flops 201326592 | bytes 12845056 | tf_op jit(solution)/shard_map/dot_general | solution.py:63
  106.3 0.8 reshape.152
  107.1 1.3 all-to-all-done.3
  108.4 4.7 %all-to-all-start.1 = ((f32[8,2,3072]{2,1,0:T(2,128)}), f32[8,2,3072]{2,1,0:T(2,128)S(1)}, u32[]{:S(2)}, u32[]{:S(2)}) async-start(f32[8,2,3072]{2,1,0:T(2,128)} %reshape.152), calls=%async_computation.1 | async-start | bytes 393216 | tf_op jit(solution)/shard_map/all_to_all | solution.py:78
  113.1 6.6 %convolution_convert_fusion = bf16[2048,3072]{1,0:T(8,128)(2,1)} fusion(bf16[16,2048]{1,0:T(8,128)(2,1)S(1)} %get-tuple-element.10, bf16[16,3072]{1,0:T(8,128)(2,1)S(1)} %reshape.156), kind=kOutput, calls=%fused_computation | convolution fusion | flops 207618048 | bytes 12746752 | tf_op jit(solution)/shard_map/rh,rd->hd/dot_general | solution.py:87
  119.8 1.1 all-to-all-done.1
  121.1 0.7 multiply_reduce_fusion
  121.8 0.7 multiply_reduce_fusion.1
  (23 shorter events, 0.4 us)
Async XLA Ops:
  7.2 1.6 %copy-start = (bf16[8,3072]{1,0:T(8,128)(2,1)S(1)}, bf16[8,3072]{1,0:T(8,128)(2,1)}, u32[]{:S(2)}) copy-start(bf16[8,3072]{1,0:T(8,128)(2,1)} %param.8) | copy-start | bytes 147460
  9.7 14.4 %all-to-all-start = ((bf16[8,2,3072]{2,1,0:T(2,128)(2,1)}), bf16[8,2,3072]{2,1,0:T(2,128)(2,1)S(1)}, u32[]{:S(2)}, u32[]{:S(2)}) async-start(bf16[8,2,3072]{2,1,0:T(2,128)(2,1)} %bitcast.1), calls=%async_computation | async-start | bytes 196608 | tf_op jit(solution)/shard_map/all_to_all | solution.py:38
  24.8 14.1 %all-to-all-start.2 = ((bf16[8,2,3072]{2,1,0:T(2,128)(2,1)}), bf16[8,2,3072]{2,1,0:T(2,128)(2,1)S(1)}, u32[]{:S(2)}, u32[]{:S(2)}) async-start(bf16[8,2,3072]{2,1,0:T(2,128)(2,1)} %bitcast.3), calls=%async_computation.2 | async-start | bytes 196608 | tf_op jit(solution)/shard_map/all_to_all | solution.py:45
  28.1 39.4 %all-reduce.3.cloned.1.call-start = ((), (), s32[]{:S(2)}) async-start(), calls=%async_computation.4 | async-start | bytes 786432 | tf_op jit(solution)/shard_map/psum | solution.py:60
  28.2 8.2 %copy-start.2 = (bf16[3072,2048]{1,0:T(8,128)(2,1)S(1)}, bf16[3072,2048]{1,0:T(8,128)(2,1)}, u32[]{:S(2)}) copy-start(bf16[3072,2048]{1,0:T(8,128)(2,1)} %param.10) | copy-start | bytes 37748740
  76.6 13.4 %slice-start = ((s8[12582912]{0:T(1024)(128)(4,1)}), s8[4194304]{0:T(1024)(128)(4,1)S(1)}, s32[]{:S(2)}) async-start(s8[12582912]{0:T(1024)(128)(4,1)} %bitcast.27), calls=%async_computation.5 | async-start | bytes 8388608
  76.6 13.4 %slice-start.1 = ((s8[12582912]{0:T(1024)(128)(4,1)}), s8[4194304]{0:T(1024)(128)(4,1)S(1)}, s32[]{:S(2)}) async-start(s8[12582912]{0:T(1024)(128)(4,1)} %bitcast.27), calls=%async_computation.6 | async-start | bytes 8388608
  83.4 6.6 %slice-start.2 = ((s8[12582912]{0:T(1024)(128)(4,1)}), s8[4194304]{0:T(1024)(128)(4,1)S(1)}, s32[]{:S(2)}) async-start(s8[12582912]{0:T(1024)(128)(4,1)} %bitcast.27), calls=%async_computation.7 | async-start | bytes 8388608
  94.2 14.2 %all-to-all-start.3 = ((f32[8,2,3072]{2,1,0:T(2,128)}), f32[8,2,3072]{2,1,0:T(2,128)S(1)}, u32[]{:S(2)}, u32[]{:S(2)}) async-start(f32[8,2,3072]{2,1,0:T(2,128)} %reshape.157), calls=%async_computation.3 | async-start | bytes 393216 | tf_op jit(solution)/shard_map/all_to_all | solution.py:79
  100.0 22.5 %copy-start.1 = (bf16[8,3072]{1,0:T(8,128)(2,1)S(1)}, bf16[8,3072]{1,0:T(8,128)(2,1)}, u32[]{:S(2)}) copy-start(bf16[8,3072]{1,0:T(8,128)(2,1)} %param.8) | copy-start | bytes 147460
  108.4 12.5 %all-to-all-start.1 = ((f32[8,2,3072]{2,1,0:T(2,128)}), f32[8,2,3072]{2,1,0:T(2,128)S(1)}, u32[]{:S(2)}, u32[]{:S(2)}) async-start(f32[8,2,3072]{2,1,0:T(2,128)} %reshape.152), calls=%async_computation.1 | async-start | bytes 393216 | tf_op jit(solution)/shard_map/all_to_all | solution.py:78
Sparse Core Ops, SparseCore 0:
  47.6 19.9 all-reduce.2
where the time goes:
time: 130 us; the launch traced here: 129 us
  matrix products  56.9 us (44%)
  waiting for transfers between devices  27.8 us (21%)
  starting transfers between devices  21.2 us (16%)
  between operations  14.1 us (11%)
  local copies, waits for them, and re-layouts  5.9 us (5%)
  other arithmetic  3.44 us (3%)
    psum x1, waiting for transfers between devices, shards(): lax.psum((pre_gate, pre_up, grad_hidden), 'tensor')  20 us
    dot_general x1, matrix products, shards(): jnp.einsum('rd,hd->rh', rows_grad, down_weight, preferred_element_type=jn...  8.59 us
    dot_general x1, matrix products, shards(): jnp.einsum('rh,dh->rd', grad_gatein, gate_weight, preferred_element_type=...  7.92 us
    all_to_all x1, starting transfers between devices, shards(): lax.all_to_all(jnp.repeat(packed_x, device_subset, axis=0), 'expert', spl...  7.25 us
    dot_general x1, matrix products, shards(): pre_up = jnp.dot(rows_x, up_weight, preferred_element_type=jnp.float32)  7.12 us
    dot_general x1, matrix products, shards(): jnp.einsum('rd,rh->dh', rows_x, grad_gatein, preferred_element_type=jnp.f...  6.81 us
    dot_general x1, matrix products, shards(): jnp.einsum('rh,rd->hd', active, rows_grad, preferred_element_type=jnp.flo...  6.61 us
    dot_general x1, matrix products, shards(): jnp.einsum('rd,rh->dh', rows_x, grad_upin, preferred_element_type=jnp.flo...  6.6 us
  transfers between devices with their start and end apart: 5, of which 4 were waited for; matrix products, arithmetic and copies ran while one was open for 20% of the time, Pallas kernels for 0%

commit v1 on v0

v1 whole, which is shorter than its diff:
```python
import functools

import jax
import jax.numpy as jnp
from jax import lax
from jax.experimental import pallas as pl
from jax.experimental.pallas import tpu as pltpu
from jax.sharding import PartitionSpec as P

MESH = pl.DeviceIdType.MESH
F32 = jnp.float32
BF16 = jnp.bfloat16

EXPERTS = 2
SLOTS = 2
PIECES = 8
RPIECES = 4
RCHUNK = 512


def iota(shape, dim):
    return lax.broadcasted_iota(jnp.int32, shape, dim)


def nn(a, b):
    return jnp.dot(a, b, preferred_element_type=F32)


def nt(a, b):
    return lax.dot_general(a, b, (((1,), (1,)), ((), ())), preferred_element_type=F32)


def tn(a, b):
    return lax.dot_general(a, b, (((0,), (0,)), ((), ())), preferred_element_type=F32)


def layer_kernel(
    n, hl, hc, tok, go, wg, wu, wd, counts, slot, gates,
    xr, gr, act, dup, dgt, mixed, gtok,
    wgv, wuv, wdv, sendx, sendg, landx, landg, gus, gur, ps, pr, rets, retl,
    wgsem, wusem, wdsem, xs, xv, gs, gv, guss, gurs, pss, prs, rss, rrs,
):
    me = lax.axis_index("expert")
    other = 1 - lax.axis_index("tensor")
    sub = n // EXPERTS
    rows = n * SLOTS
    width = tok.shape[1]
    tok_dev = tok.shape[0]
    nch = hl // hc
    nd = width // RCHUNK
    piece = width // PIECES
    rl = RCHUNK // RPIECES

    def load(hbm, vmem, sem, c, axis):
        at = pl.ds(pl.multiple_of(c * hc, hc), hc)
        view = (slice(None), at) if axis == 1 else (at, slice(None))
        return pltpu.make_async_copy(hbm.at[view], vmem.at[view], sem.at[c])

    @pl.loop(0, nch)
    def _(c):
        load(wg, wgv, wgsem, c, 1).start()
        load(wu, wuv, wusem, c, 1).start()

    @pl.loop(0, nch)
    def _(c):
        load(wd, wdv, wdsem, c, 0).start()

    barrier = pltpu.get_barrier_semaphore()

    @pl.loop(1, n)
    def _(i):
        pl.semaphore_signal(
            barrier, inc=1, device_id={"expert": lax.rem(me + i, n)}, device_id_type=MESH
        )

    pl.semaphore_signal(barrier, inc=1, device_id={"tensor": other}, device_id_type=MESH)

    srows = EXPERTS * SLOTS * PIECES
    r_i = iota((srows, tok_dev), 0)
    t_i = iota((srows, tok_dev), 1)
    pick = jnp.zeros((srows, tok_dev), F32)
    r_c = iota((srows, 1), 0)
    scale = jnp.zeros((srows, 1), F32)
    for e in range(EXPERTS):
        for s in range(SLOTS):
            q = e * SLOTS + s
            live = jnp.where(s < counts[0, e], 1.0, 0.0).astype(F32)
            pick = jnp.where((r_i // PIECES == q) & (t_i == slot[0, e, s]), live, pick)
            scale = jnp.where(r_c // PIECES == q, gates[0, e, s], scale)
    xa = jnp.zeros((srows, piece), F32)
    ga = jnp.zeros((srows, piece), F32)
    for k in range(PIECES):
        pk = jnp.where(r_i % PIECES == k, pick, 0.0).astype(BF16)
        xa = xa + nn(pk, tok[:, k * piece : (k + 1) * piece])
        ga = ga + nn(pk, go[:, k * piece : (k + 1) * piece])
    ga = ga * scale
    for e in range(EXPERTS):
        sendx[e] = xa[e * 16 : (e + 1) * 16].astype(BF16)
        sendg[e] = ga[e * 16 : (e + 1) * 16].astype(BF16)

    pl.semaphore_wait(barrier, n)

    def dispatch(buf, land, ssem, rsem, i, sending):
        peer = lax.rem(me + i, n)
        at = me if sending else peer
        return pltpu.make_async_remote_copy(
            src_ref=buf.at[peer // sub],
            dst_ref=land.at[at],
            send_sem=ssem.at[peer],
            recv_sem=rsem.at[at],
            device_id={"expert": peer},
            device_id_type=MESH,
        )

    @pl.loop(1, n)
    def _(i):
        dispatch(sendx, landx, xs, xv, i, True).start()

    @pl.loop(1, n)
    def _(i):
        dispatch(sendg, landg, gs, gv, i, True).start()

    landx[me] = sendx[me // sub]
    landg[me] = sendg[me // sub]

    d_r = iota((rows, n * 16), 0)
    d_c = iota((rows, n * 16), 1)

    def unpack(land, out):
        flat = land[...].reshape(n * 16, piece)
        for k in range(PIECES):
            sel = jnp.where(d_c == d_r * PIECES + k, 1.0, 0.0).astype(BF16)
            out[:, k * piece : (k + 1) * piece] = nn(sel, flat).astype(BF16)

    @pl.loop(1, n)
    def _(i):
        dispatch(sendx, landx, xs, xv, i, False).wait_recv()

    unpack(landx, xr)

    def swap(buf, land, ssem, rsem, c):
        return pltpu.make_async_remote_copy(
            src_ref=buf.at[c],
            dst_ref=land.at[c],
            send_sem=ssem.at[c],
            recv_sem=rsem.at[c],
            device_id={"tensor": other},
            device_id_type=MESH,
        )

    @pl.loop(0, nch)
    def _(c):
        at = pl.ds(pl.multiple_of(c * hc, hc), hc)
        load(wg, wgv, wgsem, c, 1).wait()
        gus[c, 0] = nn(xr[...], wgv[:, at])
        load(wu, wuv, wusem, c, 1).wait()
        gus[c, 1] = nn(xr[...], wuv[:, at])
        swap(gus, gur, guss, gurs, c).start()

    @pl.loop(1, n)
    def _(i):
        dispatch(sendg, landg, gs, gv, i, False).wait_recv()

    unpack(landg, gr)

    @pl.loop(0, nch)
    def _(c):
        at = pl.ds(pl.multiple_of(c * hc, hc), hc)
        load(wd, wdv, wdsem, c, 0).wait()
        ps[c] = nt(gr[...], wdv[at, :])
        swap(ps, pr, pss, prs, c).start()

    @pl.loop(0, nch)
    def _(c):
        at = pl.ds(pl.multiple_of(c * hc, hc), hc)
        swap(gus, gur, guss, gurs, c).wait_recv()
        swap(ps, pr, pss, prs, c).wait_recv()
        g = gus[c, 0] + gur[c, 0]
        u = gus[c, 1] + gur[c, 1]
        p = ps[c] + pr[c]
        sig = jax.nn.sigmoid(g)
        gsig = g * sig
        act[:, at] = (gsig * u).astype(BF16)
        dup[:, at] = (p * gsig).astype(BF16)
        dgt[:, at] = (p * u * sig * (1.0 + g * (1.0 - sig))).astype(BF16)

    m_r = iota((n * 16, rows), 0)
    m_c = iota((n * 16, rows), 1)
    home = (m_r // 16) * SLOTS + (m_r // RPIECES) % SLOTS == m_c

    def back(j, i, sending):
        peer = lax.rem(me + i, n)
        at = me if sending else peer
        return pltpu.make_async_remote_copy(
            src_ref=rets.at[j, peer],
            dst_ref=retl.at[j, at],
            send_sem=rss.at[j, peer],
            recv_sem=rrs.at[j, at],
            device_id={"expert": peer},
            device_id_type=MESH,
        )

    @pl.loop(0, nd)
    def _(j):
        at = pl.ds(pl.multiple_of(j * RCHUNK, RCHUNK), RCHUNK)
        y = nn(act[...], wdv[:, at])
        dx = nt(dgt[...], wgv[at, :]) + nt(dup[...], wuv[at, :])
        total = jnp.zeros((n * 16, rl), F32)
        for arr, val in ((0, y.astype(BF16)), (1, dx.astype(BF16))):
            for k in range(RPIECES):
                here = home & ((m_r // 8) % 2 == arr) & (m_r % RPIECES == k)
                sel = jnp.where(here, 1.0, 0.0).astype(BF16)
                total = total + nn(sel, val[:, k * rl : (k + 1) * rl])
        rets[j] = total.astype(BF16).reshape(n, 16, rl)

        @pl.loop(1, n)
        def _(i):
            back(j, i, True).start()

        retl[j, me] = rets[j, me]

    tcol = iota((tok_dev, 1), 0)
    weights = []
    for e in range(EXPERTS):
        for s in range(SLOTS):
            live = jnp.where(s < counts[0, e], 1.0, 0.0).astype(F32)
            hit = jnp.where(tcol == slot[0, e, s], live, 0.0)
            weights.append((hit * gates[0, e, s], hit))

    @pl.loop(0, nd)
    def _(j):
        @pl.loop(1, n)
        def _(i):
            back(j, i, False).wait_recv()

        sums = []
        for e in range(EXPERTS):
            sums.append(
                lax.fori_loop(
                    1,
                    sub,
                    lambda d, acc: acc + retl[j, e * sub + d].astype(F32),
                    retl[j, e * sub].astype(F32),
                )
            )
        for arr, out in ((0, mixed), (1, gtok)):
            for k in range(RPIECES):
                acc = jnp.zeros((tok_dev, rl), F32)
                for e in range(EXPERTS):
                    for s in range(SLOTS):
                        row = arr * 8 + s * RPIECES + k
                        acc = acc + weights[e * SLOTS + s][arr] * sums[e][row : row + 1, :]
                out[:, pl.ds(pl.multiple_of(j * RCHUNK + k * rl, rl), rl)] = acc

    @pl.loop(1, n)
    def _(i):
        dispatch(sendx, landx, xs, xv, i, True).wait_send()
        dispatch(sendg, landg, gs, gv, i, True).wait_send()

        @pl.loop(0, nd)
        def _(j):
            back(j, i, True).wait_send()

    @pl.loop(0, nch)
    def _(c):
        swap(gus, gur, guss, gurs, c).wait_send()
        swap(ps, pr, pss, prs, c).wait_send()


def layer(n, tokens, grad_out, wg, wu, wd, counts, slot, gates):
    tok_dev, width = tokens.shape
    hl = wg.shape[1]
    hc = min(256, hl)
    nch = hl // hc
    rows = n * SLOTS
    nd = width // RCHUNK
    rl = RCHUNK // RPIECES
    piece = width // PIECES
    vmem = pl.BlockSpec(memory_space=pltpu.VMEM)
    smem = pl.BlockSpec(memory_space=pltpu.SMEM)
    hbm = pl.BlockSpec(memory_space=pl.ANY)
    dma = pltpu.SemaphoreType.DMA
    return pl.pallas_call(
        functools.partial(layer_kernel, n, hl, hc),
        out_shape=(
            jax.ShapeDtypeStruct((rows, width), BF16),
            jax.ShapeDtypeStruct((rows, width), BF16),
            jax.ShapeDtypeStruct((rows, hl), BF16),
            jax.ShapeDtypeStruct((rows, hl), BF16),
            jax.ShapeDtypeStruct((rows, hl), BF16),
            jax.ShapeDtypeStruct((tok_dev, width), F32),
            jax.ShapeDtypeStruct((tok_dev, width), F32),
        ),
        in_specs=[vmem, vmem, hbm, hbm, hbm, smem, smem, smem],
        out_specs=(vmem,) * 7,
        scratch_shapes=[
            pltpu.VMEM((width, hl), BF16),
            pltpu.VMEM((width, hl), BF16),
            pltpu.VMEM((hl, width), BF16),
            pltpu.VMEM((EXPERTS, 16, piece), BF16),
            pltpu.VMEM((EXPERTS, 16, piece), BF16),
            pltpu.VMEM((n, 16, piece), BF16),
            pltpu.VMEM((n, 16, piece), BF16),
            pltpu.VMEM((nch, 2, rows, hc), F32),
            pltpu.VMEM((nch, 2, rows, hc), F32),
            pltpu.VMEM((nch, rows, hc), F32),
            pltpu.VMEM((nch, rows, hc), F32),
            pltpu.VMEM((nd, n, 16, rl), BF16),
            pltpu.VMEM((nd, n, 16, rl), BF16),
            dma((nch,)), dma((nch,)), dma((nch,)),
            dma((n,)), dma((n,)), dma((n,)), dma((n,)),
            dma((nch,)), dma((nch,)), dma((nch,)), dma((nch,)),
            dma((nd, n)), dma((nd, n)),
        ],
        compiler_params=pltpu.CompilerParams(
            collective_id=0, has_side_effects=True, vmem_limit_bytes=58 * 1024 * 1024
        ),
        name="layer",
    )(tokens, grad_out, wg, wu, wd, counts, slot, gates)


def grads_kernel(step_h, xr, gr, act, dup, dgt, mixed, gtok, m_out, t_out, gg, gu, gd):
    @pl.when(pl.program_id(0) == 0)
    def _():
        m_out[...] = mixed[...].astype(BF16)
        t_out[...] = gtok[...].astype(BF16)

    hl = dup.shape[1]
    x = xr[...]
    q = gr[...]
    for h in range(0, hl, step_h):
        gg[:, h : h + step_h] = tn(x, dgt[:, h : h + step_h]).astype(BF16)
        gu[:, h : h + step_h] = tn(x, dup[:, h : h + step_h]).astype(BF16)
        gd[h : h + step_h, :] = tn(act[:, h : h + step_h], q).astype(BF16)


def weight_grads(xr, gr, act, dup, dgt, mixed, gtok):
    rows, width = xr.shape
    hl = act.shape[1]
    tok_dev = mixed.shape[0]
    steps = 8
    dw = width // steps
    cols = pl.BlockSpec((rows, dw), lambda i: (0, i))
    hid = pl.BlockSpec((rows, hl), lambda i: (0, 0))
    small = pl.BlockSpec((tok_dev, width), lambda i: (0, 0))
    return pl.pallas_call(
        functools.partial(grads_kernel, min(256, hl)),
        grid=(steps,),
        out_shape=(
            jax.ShapeDtypeStruct((tok_dev, width), BF16),
            jax.ShapeDtypeStruct((tok_dev, width), BF16),
            jax.ShapeDtypeStruct((width, hl), BF16),
            jax.ShapeDtypeStruct((width, hl), BF16),
            jax.ShapeDtypeStruct((hl, width), BF16),
        ),
        in_specs=[cols, cols, hid, hid, hid, small, small],
        out_specs=(
            small,
            small,
            pl.BlockSpec((dw, hl), lambda i: (i, 0)),
            pl.BlockSpec((dw, hl), lambda i: (i, 0)),
            pl.BlockSpec((hl, dw), lambda i: (0, i)),
        ),
        compiler_params=pltpu.CompilerParams(
            dimension_semantics=("arbitrary",), vmem_limit_bytes=48 * 1024 * 1024
        ),
        name="weight_grads",
    )(xr, gr, act, dup, dgt, mixed, gtok)


def shards(tokens, grad_out, gate_weight, up_weight, down_weight, counts, slot_token, gates):
    n = lax.axis_size("expert")
    held = layer(
        n, tokens, grad_out, gate_weight, up_weight, down_weight, counts, slot_token, gates
    )
    return weight_grads(*held)


def solution(mesh):
    in_specs = (
        P(("groups", "expert"), "tensor"),
        P(("groups", "expert"), "tensor"),
        P("tensor", "expert"),
        P("tensor", "expert"),
        P("expert", "tensor"),
        P(("groups", "expert"), None),
        P(("groups", "expert"), None, None),
        P(("groups", "expert"), None, None),
    )
    out_specs = (
        P(("groups", "expert"), "tensor"),
        P(("groups", "expert"), "tensor"),
        P(("groups", "tensor"), "expert"),
        P(("groups", "tensor"), "expert"),
        P(("groups", "expert"), "tensor"),
    )
    return jax.shard_map(shards, mesh=mesh, in_specs=in_specs, out_specs=out_specs, check_vma=False)
```

time: 130 us -> 65.6 us (0.50)
  Pallas kernels: 0 us -> 58.4 us
  matrix products: 56.9 us -> 0 us
  waiting for transfers between devices: 27.8 us -> 0 us
  starting transfers between devices: 21.2 us -> 0 us
  between operations: 14.1 us -> 0.66 us
  other arithmetic: 3.44 us -> 0 us
    pallas_call x0 -> x2, Pallas kernels: none -> 58.4 us  [the longest x1 43.1 us: layer(): pl.pallas_call(functools.partial(layer_kernel, n, hl, hc), out_shape=(jax...]
    dot_general x11 -> x0, matrix products: 56.9 us -> none  [the longest x1 8.59 us: shards(): jnp.einsum('rd,hd->rh', rows_grad, down_weight, preferred_element_type=jn...]
    all_to_all x4 -> x0, starting transfers between devices: 21.1 us -> none  [the longest x1 7.25 us: shards(): lax.all_to_all(jnp.repeat(packed_x, device_subset, axis=0), 'expert', spl...]
    psum x1 -> x0, waiting for transfers between devices: 20 us -> none  [shards(): lax.psum((pre_gate, pre_up, grad_hidden), 'tensor')]
    all_to_all x4 -> x0, waiting for transfers between devices: 7.75 us -> none  [the longest x1 5.34 us: shards(): lax.all_to_all(jnp.repeat(packed_x, device_subset, axis=0), 'expert', spl...]
    unnamed x12 -> x14, local copies, waits for them, and re-layouts: 1.1 us -> 6.08 us
    convert_element_type x2 -> x0, other arithmetic: 1.83 us -> none  [the longest x1 1.11 us: shards(): grad_upin = (grad_hidden * pre_gate * gate_sig).astype(jnp.bfloat16)]
    reshape x6 -> x0, local copies, waits for them, and re-layouts: 1.71 us -> none  [the longest x1 0.8 us: shards(): back_part = back_part.reshape(holder_devices, SLOT_CAPACITY, column_range)]
  transfers between devices with their start and end apart: 5 -> 0, of which waited for: 4 -> 0; matrix products, arithmetic and copies ran while one was open for 20% -> 0% of each run, Pallas kernels for 0% -> 0%
where the time goes in v1:
time: 65.6 us; the launch traced here: 65.1 us
  Pallas kernels  58.4 us (89%)
  local copies, waits for them, and re-layouts  6.08 us (9%)
  between operations  0.66 us (1%)
    pallas_call x1, Pallas kernels, layer(): pl.pallas_call(functools.partial(layer_kernel, n, hl, hc), out_shape=(jax...  43.1 us
    pallas_call x1, Pallas kernels, weight_grads(): pl.pallas_call(functools.partial(grads_kernel, min(256, hl)), grid=(steps...  15.3 us
    unnamed x14, local copies, waits for them, and re-layouts  6.08 us

profile of v1, /device:TPU:0, one launch (start us, length us, event | category | flops | bytes accessed | tf_op | source)
XLA Modules:
  0.0 65.1 jit_solution(13069574208631064094)
XLA Ops:
  0.6 43.1 %layer.1 = (bf16[16,3072]{1,0:T(8,128)(2,1)}, bf16[16,3072]{1,0:T(8,128)(2,1)}, bf16[16,2048]{1,0:T(8,128)(2,1)}, bf16[16,2048]{1,0:T(8,128)(2,1)}, bf16[16,2048...) custom-call(bf16[8,3072]{1,0:T(8,128)(2,1)} %tok.1, bf16[8,3072]{1,0:T(8,128)(2,1)} %go.1, ...), custom_call_target="tpu_custom_call" | custom-call | tf_op jit(solution)/shard_map/layer/pallas_call | solution.py:283
  43.7 0.0 copy-start
  43.7 0.9 %copy-done = bf16[16,3072]{1,0:T(8,128)(2,1)S(1)} copy-done((bf16[16,3072]{1,0:T(8,128)(2,1)S(1)}, bf16[16,3072]{1,0:T(8,128)(2,1)}, u32[]{:S(2)}) %copy-start) | copy-done | bytes 98328
  44.6 0.0 copy-start.1
  44.6 0.9 %copy-done.1 = bf16[16,3072]{1,0:T(8,128)(2,1)S(1)} copy-done((bf16[16,3072]{1,0:T(8,128)(2,1)S(1)}, bf16[16,3072]{1,0:T(8,128)(2,1)}, u32[]{:S(2)}) %copy-start.1) | copy-done | bytes 98328
  45.5 0.0 copy-start.2
  45.5 0.9 %copy-done.2 = f32[8,3072]{1,0:T(8,128)S(1)} copy-done((f32[8,3072]{1,0:T(8,128)S(1)}, f32[8,3072]{1,0:T(8,128)}, u32[]{:S(2)}) %copy-start.2) | copy-done | bytes 98328
  46.4 0.0 copy-start.3
  46.4 0.9 %copy-done.3 = f32[8,3072]{1,0:T(8,128)S(1)} copy-done((f32[8,3072]{1,0:T(8,128)S(1)}, f32[8,3072]{1,0:T(8,128)}, u32[]{:S(2)}) %copy-start.3) | copy-done | bytes 98328
  47.3 0.0 copy-start.4
  47.3 0.8 %copy-done.4 = bf16[16,2048]{1,0:T(8,128)(2,1)S(1)} copy-done((bf16[16,2048]{1,0:T(8,128)(2,1)S(1)}, bf16[16,2048]{1,0:T(8,128)(2,1)}, u32[]{:S(2)}) %copy-start.4) | copy-done | bytes 65560
  48.1 0.0 copy-start.5
  48.1 0.8 %copy-done.5 = bf16[16,2048]{1,0:T(8,128)(2,1)S(1)} copy-done((bf16[16,2048]{1,0:T(8,128)(2,1)S(1)}, bf16[16,2048]{1,0:T(8,128)(2,1)}, u32[]{:S(2)}) %copy-start.5) | copy-done | bytes 65560
  49.0 0.0 copy-start.6
  49.0 0.8 %copy-done.6 = bf16[16,2048]{1,0:T(8,128)(2,1)S(1)} copy-done((bf16[16,2048]{1,0:T(8,128)(2,1)S(1)}, bf16[16,2048]{1,0:T(8,128)(2,1)}, u32[]{:S(2)}) %copy-start.6) | copy-done | bytes 65560
  49.8 15.3 %weight_grads.1 = (bf16[8,3072]{1,0:T(8,128)(2,1)}, bf16[8,3072]{1,0:T(8,128)(2,1)}, bf16[3072,2048]{1,0:T(8,128)(2,1)}, bf16[3072,2048]{1,0:T(8,128)(2,1)}, bf16[2048,3072]{1,0:T(8,128)(2,1)}) custom-call(bf16[16,3072]{1,0:T(8,128)(2,1)S(1)} %copy-done, bf16[16,3072]{1,0:T(8,128)(2,1)S(1)} %copy-done.1, bf16[16,2048]{1,0:T(8,128)(2,1)S(1)} %copy-done.4, ...), custom_call_target="tpu_custom_call" | custom-call | tf_op jit(solution)/shard_map/weight_grads/pallas_call | solution.py:346
Async XLA Ops:
  43.7 0.9 %copy-start = (bf16[16,3072]{1,0:T(8,128)(2,1)S(1)}, bf16[16,3072]{1,0:T(8,128)(2,1)}, u32[]{:S(2)}) copy-start(bf16[16,3072]{1,0:T(8,128)(2,1)} %get-tuple-element.12.xr) | copy-start | bytes 294916
  44.6 0.9 %copy-start.1 = (bf16[16,3072]{1,0:T(8,128)(2,1)S(1)}, bf16[16,3072]{1,0:T(8,128)(2,1)}, u32[]{:S(2)}) copy-start(bf16[16,3072]{1,0:T(8,128)(2,1)} %get-tuple-element.13.gr) | copy-start | bytes 294916
  45.5 0.9 %copy-start.2 = (f32[8,3072]{1,0:T(8,128)S(1)}, f32[8,3072]{1,0:T(8,128)}, u32[]{:S(2)}) copy-start(f32[8,3072]{1,0:T(8,128)} %get-tuple-element.17.mixed) | copy-start | bytes 294916
  46.4 0.9 %copy-start.3 = (f32[8,3072]{1,0:T(8,128)S(1)}, f32[8,3072]{1,0:T(8,128)}, u32[]{:S(2)}) copy-start(f32[8,3072]{1,0:T(8,128)} %get-tuple-element.18.gtok) | copy-start | bytes 294916
  47.3 0.8 %copy-start.4 = (bf16[16,2048]{1,0:T(8,128)(2,1)S(1)}, bf16[16,2048]{1,0:T(8,128)(2,1)}, u32[]{:S(2)}) copy-start(bf16[16,2048]{1,0:T(8,128)(2,1)} %get-tuple-element.14.act) | copy-start | bytes 196612
  48.1 0.8 %copy-start.5 = (bf16[16,2048]{1,0:T(8,128)(2,1)S(1)}, bf16[16,2048]{1,0:T(8,128)(2,1)}, u32[]{:S(2)}) copy-start(bf16[16,2048]{1,0:T(8,128)(2,1)} %get-tuple-element.15.dup) | copy-start | bytes 196612
  49.0 0.8 %copy-start.6 = (bf16[16,2048]{1,0:T(8,128)(2,1)S(1)}, bf16[16,2048]{1,0:T(8,128)(2,1)}, u32[]{:S(2)}) copy-start(bf16[16,2048]{1,0:T(8,128)(2,1)} %get-tuple-element.16.dgt) | copy-start | bytes 196612

commit v2 on v1

--- a/solution.py
+++ b/solution.py
@@ -37,7 +37,7 @@
 def layer_kernel(
     n, hl, hc, tok, go, wg, wu, wd, counts, slot, gates,
     xr, gr, act, dup, dgt, mixed, gtok,
-    wgv, wuv, wdv, sendx, sendg, landx, landg, gus, gur, ps, pr, rets, retl,
+    wgv, wuv, wdv, home, sendx, sendg, landx, landg, gus, gur, ps, pr, rets, retl,
     wgsem, wusem, wdsem, xs, xv, gs, gv, guss, gurs, pss, prs, rss, rrs,
 ):
     me = lax.axis_index("expert")
@@ -76,23 +76,28 @@
     pl.semaphore_signal(barrier, inc=1, device_id={"tensor": other}, device_id_type=MESH)
 
     srows = EXPERTS * SLOTS * PIECES
-    r_i = iota((srows, tok_dev), 0)
-    t_i = iota((srows, tok_dev), 1)
-    pick = jnp.zeros((srows, tok_dev), F32)
+    r_i = iota((srows, PIECES * tok_dev), 0)
+    c_i = iota((srows, PIECES * tok_dev), 1)
+    same = r_i % PIECES == c_i // tok_dev
+    pick = jnp.zeros((srows, PIECES * tok_dev), F32)
     r_c = iota((srows, 1), 0)
     scale = jnp.zeros((srows, 1), F32)
     for e in range(EXPERTS):
         for s in range(SLOTS):
             q = e * SLOTS + s
             live = jnp.where(s < counts[0, e], 1.0, 0.0).astype(F32)
-            pick = jnp.where((r_i // PIECES == q) & (t_i == slot[0, e, s]), live, pick)
+            hit = same & (r_i // PIECES == q) & (c_i % tok_dev == slot[0, e, s])
+            pick = jnp.where(hit, live, pick)
             scale = jnp.where(r_c // PIECES == q, gates[0, e, s], scale)
-    xa = jnp.zeros((srows, piece), F32)
-    ga = jnp.zeros((srows, piece), F32)
-    for k in range(PIECES):
-        pk = jnp.where(r_i % PIECES == k, pick, 0.0).astype(BF16)
-        xa = xa + nn(pk, tok[:, k * piece : (k + 1) * piece])
-        ga = ga + nn(pk, go[:, k * piece : (k + 1) * piece])
+    pick = pick.astype(BF16)
+
+    def stack(ref):
+        wide = ref[...].astype(F32)
+        parts = [wide[:, k * piece : (k + 1) * piece] for k in range(PIECES)]
+        return jnp.concatenate(parts, axis=0).astype(BF16)
+
+    xa = nn(pick, stack(tok))
+    ga = nn(pick, stack(go))
     ga = ga * scale
     for e in range(EXPERTS):
         sendx[e] = xa[e * 16 : (e + 1) * 16].astype(BF16)
@@ -123,14 +128,19 @@
     landx[me] = sendx[me // sub]
     landg[me] = sendg[me // sub]
 
-    d_r = iota((rows, n * 16), 0)
-    d_c = iota((rows, n * 16), 1)
+    d_r = iota((PIECES * rows, n * 16), 0)
+    d_c = iota((PIECES * rows, n * 16), 1)
+    spread = (d_c == (d_r % rows) * PIECES + d_r // rows).astype(F32).astype(BF16)
+    m_r = iota((n * 16, 2 * RPIECES * rows), 0)
+    m_c = iota((n * 16, 2 * RPIECES * rows), 1)
+    m_row = (m_r // 16) * SLOTS + (m_r // RPIECES) % SLOTS
+    m_part = ((m_r // 8) % 2) * RPIECES + m_r % RPIECES
+    home[...] = (m_c == m_part * rows + m_row).astype(F32).astype(BF16)
 
     def unpack(land, out):
-        flat = land[...].reshape(n * 16, piece)
+        moved = nn(spread, land[...].reshape(n * 16, piece)).astype(BF16)
         for k in range(PIECES):
-            sel = jnp.where(d_c == d_r * PIECES + k, 1.0, 0.0).astype(BF16)
-            out[:, k * piece : (k + 1) * piece] = nn(sel, flat).astype(BF16)
+            out[:, k * piece : (k + 1) * piece] = moved[k * rows : (k + 1) * rows]
 
     @pl.loop(1, n)
     def _(i):
@@ -184,10 +194,6 @@
         dup[:, at] = (p * gsig).astype(BF16)
         dgt[:, at] = (p * u * sig * (1.0 + g * (1.0 - sig))).astype(BF16)
 
-    m_r = iota((n * 16, rows), 0)
-    m_c = iota((n * 16, rows), 1)
-    home = (m_r // 16) * SLOTS + (m_r // RPIECES) % SLOTS == m_c
-
     def back(j, i, sending):
         peer = lax.rem(me + i, n)
         at = me if sending else peer
@@ -205,12 +211,9 @@
         at = pl.ds(pl.multiple_of(j * RCHUNK, RCHUNK), RCHUNK)
         y = nn(act[...], wdv[:, at])
         dx = nt(dgt[...], wgv[at, :]) + nt(dup[...], wuv[at, :])
-        total = jnp.zeros((n * 16, rl), F32)
-        for arr, val in ((0, y.astype(BF16)), (1, dx.astype(BF16))):
-            for k in range(RPIECES):
-                here = home & ((m_r // 8) % 2 == arr) & (m_r % RPIECES == k)
-                sel = jnp.where(here, 1.0, 0.0).astype(BF16)
-                total = total + nn(sel, val[:, k * rl : (k + 1) * rl])
+        vals = (y.astype(BF16), dx.astype(BF16))
+        parts = [v[:, k * rl : (k + 1) * rl] for v in vals for k in range(RPIECES)]
+        total = nn(home[...], jnp.concatenate(parts, axis=0))
         rets[j] = total.astype(BF16).reshape(n, 16, rl)
 
         @pl.loop(1, n)
@@ -270,7 +273,7 @@
 def layer(n, tokens, grad_out, wg, wu, wd, counts, slot, gates):
     tok_dev, width = tokens.shape
     hl = wg.shape[1]
-    hc = min(256, hl)
+    hc = min(512, hl)
     nch = hl // hc
     rows = n * SLOTS
     nd = width // RCHUNK
@@ -297,6 +300,7 @@
             pltpu.VMEM((width, hl), BF16),
             pltpu.VMEM((width, hl), BF16),
             pltpu.VMEM((hl, width), BF16),
+            pltpu.VMEM((n * 16, 2 * RPIECES * rows), BF16),
             pltpu.VMEM((EXPERTS, 16, piece), BF16),
             pltpu.VMEM((EXPERTS, 16, piece), BF16),
             pltpu.VMEM((n, 16, piece), BF16),
@@ -362,7 +366,7 @@
             pl.BlockSpec((hl, dw), lambda i: (0, i)),
         ),
         compiler_params=pltpu.CompilerParams(
-            dimension_semantics=("arbitrary",), vmem_limit_bytes=48 * 1024 * 1024
+            dimension_semantics=("arbitrary",), vmem_limit_bytes=60 * 1024 * 1024
         ),
         name="weight_grads",
     )(xr, gr, act, dup, dgt, mixed, gtok)

time: 65.6 us -> 54.2 us (0.83)
  local copies, waits for them, and re-layouts: 6.08 us -> 0 us
  Pallas kernels: 58.4 us -> 53.3 us
    pallas_call x1, Pallas kernels: 43.1 us -> 36.9 us  [layer(): pl.pallas_call(functools.partial(layer_kernel, n, hl, hc), out_shape=(jax...]
    unnamed x14 -> x0, local copies, waits for them, and re-layouts: 6.08 us -> none
    pallas_call x1, Pallas kernels: 15.3 us -> 16.4 us  [weight_grads(): pl.pallas_call(functools.partial(grads_kernel, min(256, hl)), grid=(steps...]
where the time goes in v2:
time: 54.2 us; the launch traced here: 53.9 us
  Pallas kernels  53.3 us (98%)
  between operations  0.64 us (1%)
    pallas_call x1, Pallas kernels, layer(): pl.pallas_call(functools.partial(layer_kernel, n, hl, hc), out_shape=(jax...  36.9 us
    pallas_call x1, Pallas kernels, weight_grads(): pl.pallas_call(functools.partial(grads_kernel, min(256, hl)), grid=(steps...  16.4 us

profile of v2, /device:TPU:0, one launch (start us, length us, event | category | flops | bytes accessed | tf_op | source)
XLA Modules:
  0.0 53.9 jit_solution(16343823508909370811)
XLA Ops:
  0.6 36.9 %layer.1 = (bf16[16,3072]{1,0:T(8,128)(2,1)}, bf16[16,3072]{1,0:T(8,128)(2,1)}, bf16[16,2048]{1,0:T(8,128)(2,1)}, bf16[16,2048]{1,0:T(8,128)(2,1)}, bf16[16,2048...) custom-call(bf16[8,3072]{1,0:T(8,128)(2,1)} %tok.1, bf16[8,3072]{1,0:T(8,128)(2,1)} %go.1, ...), custom_call_target="tpu_custom_call" | custom-call | tf_op jit(solution)/shard_map/layer/pallas_call | solution.py:286
  37.5 16.4 %weight_grads.1 = (bf16[8,3072]{1,0:T(8,128)(2,1)}, bf16[8,3072]{1,0:T(8,128)(2,1)}, bf16[3072,2048]{1,0:T(8,128)(2,1)}, bf16[3072,2048]{1,0:T(8,128)(2,1)}, bf16[2048,3072]{1,0:T(8,128)(2,1)}) custom-call(bf16[16,3072]{1,0:T(8,128)(2,1)} %get-tuple-element.12.xr, bf16[16,3072]{1,0:T(8,128)(2,1)} %get-tuple-element.13.gr, ...), custom_call_target="tpu_custom_call" | custom-call | tf_op jit(solution)/shard_map/weight_grads/pallas_call | solution.py:350

commit v3 on v2

--- a/solution.py
+++ b/solution.py
@@ -15,7 +15,7 @@
 SLOTS = 2
 PIECES = 8
 RPIECES = 4
-RCHUNK = 512
+RCHUNK = 1024
 
 
 def iota(shape, dim):
@@ -273,7 +273,7 @@
 def layer(n, tokens, grad_out, wg, wu, wd, counts, slot, gates):
     tok_dev, width = tokens.shape
     hl = wg.shape[1]
-    hc = min(512, hl)
+    hc = min(1024, hl)
     nch = hl // hc
     rows = n * SLOTS
     nd = width // RCHUNK

time: 54.2 us -> 52 us (0.959)
  Pallas kernels: 53.3 us -> 51.2 us
    pallas_call x1, Pallas kernels: 36.9 us -> 34.7 us  [layer(): pl.pallas_call(functools.partial(layer_kernel, n, hl, hc), out_shape=(jax...]
where the time goes in v3:
time: 52 us; the launch traced here: 51.8 us
  Pallas kernels  51.2 us (98%)
  between operations  0.64 us (1%)
    pallas_call x1, Pallas kernels, layer(): pl.pallas_call(functools.partial(layer_kernel, n, hl, hc), out_shape=(jax...  34.7 us
    pallas_call x1, Pallas kernels, weight_grads(): pl.pallas_call(functools.partial(grads_kernel, min(256, hl)), grid=(steps...  16.4 us

profile of v3, /device:TPU:0, one launch (start us, length us, event | category | flops | bytes accessed | tf_op | source)
XLA Modules:
  0.0 51.8 jit_solution(5051931922895121817)
XLA Ops:
  0.6 34.7 %layer.1 = (bf16[16,3072]{1,0:T(8,128)(2,1)}, bf16[16,3072]{1,0:T(8,128)(2,1)}, bf16[16,2048]{1,0:T(8,128)(2,1)}, bf16[16,2048]{1,0:T(8,128)(2,1)}, bf16[16,2048...) custom-call(bf16[8,3072]{1,0:T(8,128)(2,1)} %tok.1, bf16[8,3072]{1,0:T(8,128)(2,1)} %go.1, ...), custom_call_target="tpu_custom_call" | custom-call | tf_op jit(solution)/shard_map/layer/pallas_call | solution.py:286
  35.4 16.4 %weight_grads.1 = (bf16[8,3072]{1,0:T(8,128)(2,1)}, bf16[8,3072]{1,0:T(8,128)(2,1)}, bf16[3072,2048]{1,0:T(8,128)(2,1)}, bf16[3072,2048]{1,0:T(8,128)(2,1)}, bf16[2048,3072]{1,0:T(8,128)(2,1)}) custom-call(bf16[16,3072]{1,0:T(8,128)(2,1)} %get-tuple-element.12.xr, bf16[16,3072]{1,0:T(8,128)(2,1)} %get-tuple-element.13.gr, ...), custom_call_target="tpu_custom_call" | custom-call | tf_op jit(solution)/shard_map/weight_grads/pallas_call | solution.py:350
